TPU v7x, 32 devices: a whole 2x2x4 slice. The times are simulated.
32 devices in a mesh: parts: 2 (over y), chan: 4 (over z), grp: 2 (over x), tpl: 2 (over core).
Axes of the slice: x: 2, y: 2, z: 4, core: 2. Of those that a mesh axis runs over, the one named last changes fastest.
Arguments:
- records: bfloat16 [64, 32768], P(None, ('parts', 'chan', 'grp')), parts along dimension 1, may hold values from -54 to 54
- fir: bfloat16 [32], replicated, may hold values from -1 to 1
- templates: bfloat16 [48, 64, 128], P('tpl', ('chan', 'grp')), may hold values from -0.09375 to 0.09375
- channel_sel: int32 [48, 64], P('tpl', ('chan', 'grp')), may hold values 0 or 1
- moveout: int32 [48, 64], P('tpl', ('chan', 'grp')), may hold values from 0 to 127
- alive: int32 [64], P(('chan', 'grp')), may hold values 0 or 1
Outputs:
- stack: float32 [48, 32768], P('tpl', ('parts', 'chan')), parts along dimension 1
There are 2 independent parts, one for each index of `parts`. A program takes and returns all parts, laid end to end along the dimension named above; an argument that names none is the same for every part. Nothing has to cross between parts.
All inputs are finite; a program needn't handle non-finite values. No bound on the sum of `channel_sel` or of `alive` on one device may be relied on, other than what follows from the above.
Results may differ from a plain program's by a relative error of at most 0.0029.
Values may be sent and summed in bfloat16 or wider, within the bound.
A program may use at most 64 MiB of HBM per device.

v0:
```python
import jax
import jax.numpy as jnp
from jax import lax
from jax.sharding import PartitionSpec as P

MMAX = 128


tile_len = 128
small_eps = 1e-06


def whiten(signal, fir):
    chan_rows, sample_count = signal.shape
    block_count = sample_count // tile_len
    blocks = signal.reshape(chan_rows, block_count, tile_len)
    earlier = jnp.concatenate(
        [jnp.zeros((chan_rows, 1, tile_len), signal.dtype), blocks[:, :-1]], axis=1
    )
    paired = jnp.concatenate([earlier, blocks], axis=2)
    source_pos = jnp.arange(2 * tile_len, dtype=jnp.int32)[:, None]
    target_pos = jnp.arange(tile_len, dtype=jnp.int32)[None, :]
    tap_lag = target_pos + tile_len - source_pos
    tap_count = fir.shape[0]
    tap_index = jnp.arange(tap_count, dtype=jnp.int32)
    hits = tap_lag[:, :, None] == tap_index[None, None, :]
    filter_matrix = jnp.sum(
        jnp.where(hits, fir.astype(jnp.float32)[None, None, :], jnp.zeros((), jnp.float32)), axis=2
    ).astype(jnp.bfloat16)
    filtered = jnp.einsum("cbi,ir->cbr", paired, filter_matrix, preferred_element_type=jnp.float32)
    filtered = filtered.reshape(chan_rows, sample_count)
    power = jnp.mean(filtered * filtered, axis=1, keepdims=True)
    return (filtered * lax.rsqrt(power + small_eps)).astype(jnp.bfloat16)


def correlate(whitened, templates, channel_sel, moveout, alive):
    tpl_count, chan_rows, tap_count = templates.shape
    extended = tap_count + MMAX
    keep_mask = (channel_sel * alive[None, :]).astype(jnp.bfloat16)
    weighted = templates * keep_mask[:, :, None]
    lag_grid = (
        jnp.arange(extended, dtype=jnp.int32)[:, None]
        - jnp.arange(tap_count, dtype=jnp.int32)[None, :]
    )
    selector = (lag_grid[None, None, :, :] == moveout[:, :, None, None]).astype(jnp.bfloat16)
    shifted_tpl = jnp.einsum(
        "kcl,kcel->kce", weighted, selector, preferred_element_type=jnp.float32
    ).astype(jnp.bfloat16)
    stack = lax.conv_general_dilated(
        whitened[None],
        shifted_tpl,
        window_strides=(1,),
        padding=((0, extended - 1),),
        dimension_numbers=("NCH", "OIH", "NCH"),
        preferred_element_type=jnp.float32,
    )
    return stack[0]


def body(records, fir, templates, channel_sel, moveout, alive):
    local_rows = lax.all_to_all(records, ("chan", "grp"), split_axis=0, concat_axis=1, tiled=True)
    whitened = whiten(local_rows, fir)
    partial_stack = correlate(whitened, templates, channel_sel, moveout, alive)
    summed_part = lax.psum_scatter(partial_stack, "chan", scatter_dimension=1, tiled=True)
    return lax.psum(summed_part, "grp")


def solution(mesh):
    in_specs = (
        P(None, ("parts", "chan", "grp")),
        P(),
        P("tpl", ("chan", "grp"), None),
        P("tpl", ("chan", "grp")),
        P("tpl", ("chan", "grp")),
        P(("chan", "grp")),
    )
    out_specs = P("tpl", ("parts", "chan"))
    return jax.shard_map(body, mesh=mesh, in_specs=in_specs, out_specs=out_specs, check_vma=False)
```

profile of v0, /device:TPU:14, one launch (start us, length us, event | category | flops | bytes accessed | tf_op | source)
XLA Modules:
  0.0 952.2 jit_solution(7759543912762481530)
XLA Ops:
  6.5 0.0 copy-start
  6.5 6.4 all-to-all-start
  12.9 0.0 reduce-scatter.2.cloned.1.call-start
  12.9 0.8 multiply_convert_fusion.1
  13.7 0.1 copy.26
  13.8 0.8 copy.27
  14.5 0.9 multiply_bitcast_fusion
  15.4 3.9 fusion
  19.3 0.0 copy-done
  19.4 0.4 copy.30
  19.8 1.5 select_reduce_fusion
  21.2 0.0 all-to-all-done
  21.2 0.2 copy.23
  21.4 0.1 reshape.90
  21.5 0.4 multiply_reduce_fusion
  22.0 0.1 reshape.91
  22.1 0.1 fusion.22
  22.2 0.5 reshape.94
  22.7 4.4 copy.25
  27.1 1.2 slice.7
  28.3 0.0 copy-start.1
  28.3 11.6 %fusion.35 = bf16[8,8,2335]{0,1,2:T(8,128)(2,1)S(1)} fusion(bf16[8,1,7,255]{0,2,3,1:T(8,128)(2,1)S(1)} %slice.7, bf16[8,1,8,2080]{0,2,3,1:T(8,128)(2,1)} %copy.25), kind=kLoop, calls=%fused_computation.7.clone.clone.clone.clone.1 | loop fusion | flops 896640 | bytes 593680 | tf_op jit(solution)/shard_map/conv_general_dilated | solution.py:49
  39.9 0.0 copy-done.1
  39.9 833.6 %broadcast_select_fusion = f32[8,2080,24]{2,0,1:T(8,128)} fusion(pred[8,2080]{0,1:T(8,128)(4,1)S(1)} %bitcast.37, bf16[24,8,1,256]{0,1,3,2:T(8,128)(2,1)S(1)} %copy.30, bf16[8,8,2335]{0,1,2:T(8,128)(2,1)S(1)} %fusion.35), kind=kOutput, calls=%fused_computation.12 | convolution fusion | flops 1636177920 | bytes 2011264 | tf_op jit(solution)/shard_map/conv_general_dilated | solution.py:49
  873.5 5.8 copy.28
  879.3 0.5 reshape.98
  879.9 1.3 slice_bitcast_fusion
  881.1 0.0 reduce-scatter.2.cloned.1.call-update
  881.1 0.0 all-reduce.3.cloned.1.call-start
  881.2 35.2 %reduce-scatter.2.cloned.1.call-done = f32[24,4096]{1,0:T(8,128)} async-done(((f32[24,16384]{1,0:T(8,128)}), f32[24,4096]{1,0:T(8,128)}) %reduce-scatter.2.cloned.1.call-update) | async-done | bytes 393232 | tf_op jit(solution)/shard_map/reduce_scatter | solution.py:64
  916.4 0.0 all-reduce.3.cloned.1.call-update
  916.4 27.2 %all-reduce.3.cloned.1.call-done = f32[24,4096]{1,0:T(8,128)} async-done(((f32[24,4096]{1,0:T(8,128)}), f32[24,4096]{1,0:T(8,128)}) %all-reduce.3.cloned.1.call-update) | async-done | bytes 393232 | tf_op jit(solution)/shard_map/psum | solution.py:65
  943.6 1.8 copy.34
  (6 shorter events, 0.1 us)
Async XLA Ops:
  6.5 12.8 %copy-start = (bf16[32]{0:T(256)(128)(2,1)S(1)}, bf16[32]{0:T(256)(128)(2,1)}, u32[]{:S(2)}) copy-start(bf16[32]{0:T(256)(128)(2,1)} %param.7) | copy-start | bytes 196
  6.5 14.7 %all-to-all-start = ((bf16[8,8,2048]{2,1,0:T(8,128)(2,1)}), bf16[8,8,2048]{2,1,0:T(8,128)(2,1)S(1)}, u32[]{:S(2)}, u32[]{:S(2)}) async-start(bf16[8,8,2048]{2,1,0:T(8,128)(2,1)} %bitcast.35), calls=%async_computation | async-start | bytes 524288 | tf_op jit(solution)/shard_map/all_to_all | solution.py:61
  12.9 903.5 %reduce-scatter.2.cloned.1.call-start = ((), (), s32[]{:S(2)}) async-start(), calls=%async_computation.2 | async-start | bytes 1966080 | tf_op jit(solution)/shard_map/reduce_scatter | solution.py:64
  28.3 11.6 %copy-start.1 = (pred[8,2080]{0,1:T(32,128)(4,1)S(1)}, pred[8,2080]{0,1:T(32,128)(4,1)}, u32[]{:S(2)}) copy-start(pred[8,2080]{0,1:T(32,128)(4,1)} %constant.17) | copy-start | bytes 49924
  881.1 62.4 %all-reduce.3.cloned.1.call-start = ((), (), s32[]{:S(2)}) async-start(), calls=%async_computation.3 | async-start | bytes 786432 | tf_op jit(solution)/shard_map/psum | solution.py:65
Sparse Core Ops, SparseCore 0:
  881.3 35.0 reduce-scatter.1
  918.6 24.8 all-reduce.2
where the time goes:
time: 955 us; the launch traced here: 952 us
  matrix products  838 us (88%)
  waiting for transfers between devices  62.4 us (7%)
  local copies, waits for them, and re-layouts  17.1 us (2%)
  other arithmetic  14.8 us (2%)
  between operations  13.5 us (1%)
    conv_general_dilated x1, matrix products, correlate(): lax.conv_general_dilated(whitened[None], shifted_tpl, window_strides=(1,)...  834 us
    reduce_scatter x1, waiting for transfers between devices, body(): lax.psum_scatter(partial_stack, 'chan', scatter_dimension=1, tiled=True)  35.2 us
    psum x1, waiting for transfers between devices, body(): return lax.psum(summed_part, 'grp')  27.2 us
  transfers between devices with their start and end apart: 3, of which 2 were waited for; matrix products, arithmetic and copies ran while one was open for 1% of the time, Pallas kernels for 0%

commit v1 on v0

v1 whole, which is shorter than its diff:
```python
import jax
import jax.numpy as jnp
from jax import lax
from jax.sharding import PartitionSpec as P

axes = ("chan", "grp")
stride = 8
extended = 256
lags = extended + stride
small_eps = 1e-06
group_rows = 64


def filter_matrix(fir):
    lag = jnp.arange(128)[None, :] + 128 - jnp.arange(256)[:, None]
    hits = lag[:, :, None] == jnp.arange(fir.shape[0])[None, None, :]
    return jnp.sum(jnp.where(hits, fir.astype(jnp.float32), 0.0), axis=2).astype(jnp.bfloat16)


def shift_templates(templates, channel_sel, moveout, alive):
    keep = (channel_sel * alive[None, :]).astype(jnp.bfloat16)
    rows = jnp.pad(templates * keep[:, :, None], ((0, 0), (0, 0), (0, 128)))
    for bit in range(7):
        moved = jnp.pad(rows, ((0, 0), (0, 0), (1 << bit, 0)))[:, :, :extended]
        rows = jnp.where(((moveout >> bit) & 1)[:, :, None] == 1, moved, rows)
    return rows


def time_split(records, fir, templates, channel_sel, moveout, alive, chan, grp):
    chans, length = records.shape
    count = chan * grp
    me = lax.axis_index(axes)
    before = lax.ppermute(records[:, length - 128:], axes, [(i, i + 1) for i in range(count - 1)])
    after = lax.ppermute(records[:, :extended], axes, [(i + 1, i) for i in range(count - 1)])
    shifted = shift_templates(templates, channel_sel, moveout, alive)
    shifted = lax.all_gather(shifted, axes, axis=1, tiled=True)
    signal = jnp.concatenate([before, records, after], axis=1)
    total = length + extended
    blocks = signal.reshape(chans, total // 128 + 1, 128)
    paired = jnp.concatenate([blocks[:, :-1], blocks[:, 1:]], axis=2)
    filtered = jnp.einsum("cbi,ir->cbr", paired, filter_matrix(fir), preferred_element_type=jnp.float32)
    filtered = filtered.reshape(chans, total)
    own = filtered[:, :length]
    power = lax.psum(jnp.sum(own * own, axis=1, keepdims=True), axes) / (length * count)
    inside = (jnp.arange(total) < length) | (me < count - 1)
    whitened = jnp.where(inside[None], filtered * lax.rsqrt(power + small_eps), 0.0).astype(jnp.bfloat16)
    steps = length // stride

    def part(wave, tpl):
        cells = wave.reshape(wave.shape[0], total // stride, stride)
        left = jnp.stack([cells[:, j:j + steps] for j in range(lags // stride)], axis=1)
        right = jnp.stack([jnp.pad(tpl, ((0, 0), (0, 0), (r, stride - r))) for r in range(stride)])
        right = right.reshape(stride, tpl.shape[0], tpl.shape[1], lags // stride, stride)
        return jnp.einsum("cjbs,rkcjs->kbr", left, right, preferred_element_type=jnp.float32)

    groups = chans // group_rows
    if groups == 1:
        stack = part(whitened, shifted)
    else:
        waves = whitened.reshape(groups, group_rows, total)
        tpls = shifted.reshape(-1, groups, group_rows, extended).transpose(1, 0, 2, 3)
        stack = jnp.zeros((shifted.shape[0], steps, stride), jnp.float32)
        stack = lax.scan(lambda acc, x: (acc + part(*x), None), stack, (waves, tpls))[0]
    stack = stack.reshape(shifted.shape[0], length)
    return lax.all_gather(stack, "grp", axis=1, tiled=True)


def solution(mesh):
    chan, grp = mesh.shape["chan"], mesh.shape["grp"]

    def body(*args):
        return time_split(*args, chan, grp)

    in_specs = (
        P(None, ("parts", "chan", "grp")),
        P(),
        P("tpl", ("chan", "grp"), None),
        P("tpl", ("chan", "grp")),
        P("tpl", ("chan", "grp")),
        P(("chan", "grp")),
    )
    out_specs = P("tpl", ("parts", "chan"))
    return jax.shard_map(body, mesh=mesh, in_specs=in_specs, out_specs=out_specs, check_vma=False)
```

time: 955 us -> 124 us (0.13)
  the two profiles are of different devices: /device:TPU:14 before, /device:TPU:0 now
where the time goes in v1:
time: 124 us
  blocking collectives  68.7 us (55%)
  local copies, waits for them, and re-layouts  38 us (31%)
  starting transfers between devices  6.74 us (5%)
  other arithmetic  5.96 us (5%)
  matrix products  3.99 us (3%)
    all_gather x1, blocking collectives, time_split(): shifted = lax.all_gather(shifted, axes, axis=1, tiled=True)  32.9 us
    unnamed x50, local copies, waits for them, and re-layouts  21.2 us
    psum x1, blocking collectives, time_split(): lax.psum(jnp.sum(own * own, axis=1, keepdims=True), axes) / (length * count)  20.4 us
    all_gather x1, blocking collectives, time_split(): return lax.all_gather(stack, 'grp', axis=1, tiled=True)  15.5 us
    pad x1, local copies, waits for them, and re-layouts, part(): jnp.pad(tpl, ((0, 0), (0, 0), (r, stride - r)))  9.82 us
    ppermute x1, starting transfers between devices, time_split(): lax.ppermute(records[:, length - 128:], axes, [(i, i + 1) for i in range(...  5.46 us
    dot_general x1, matrix products, part(): jnp.einsum('cjbs,rkcjs->kbr', left, right, preferred_element_type=jnp.flo...  3.69 us
  transfers between devices with their start and end apart: 2, of which 0 were waited for; matrix products, arithmetic and copies ran while one was open for 28% of the time, Pallas kernels for 0%

profile of v1, /device:TPU:0, one launch (start us, length us, event | category | flops | bytes accessed | tf_op | source)
XLA Modules:
  0.0 123.8 jit_solution(2870272245873950611)
XLA Ops:
  0.0 0.8 slice.143
  0.8 1.3 %collective-permute-start.1 = (bf16[64,256]{1,0:T(8,128)(2,1)S(1)}, bf16[64,256]{1,0:T(8,128)(2,1)S(1)}, u32[]{:S(2)}, u32[]{:S(2)}) collective-permute-start(bf16[64,256]{1,0:T(8,128)(2,1)S(1)} %slice.143), channel_id=1, source_target_pairs={{2,0},{4,2},{6,4},{8,6},{10,8},{12,10},{14,12},{3,1},{5,3},{7,5},{... | collective-permute-start | bytes 98312 | tf_op jit(solution)/shard_map/ppermute | solution.py:34
  2.0 0.7 slice.142
  2.8 5.5 %collective-permute-start = (bf16[64,128]{1,0:T(8,128)(2,1)S(1)}, bf16[64,128]{1,0:T(8,128)(2,1)S(1)}, u32[]{:S(2)}, u32[]{:S(2)}) collective-permute-start(bf16[64,128]{1,0:T(8,128)(2,1)S(1)} %slice.142), channel_id=1, source_target_pairs={{0,2},{2,4},{4,6},{6,8},{8,10},{10,12},{12,14},{1,3},{3,5},{5,7},{... | collective-permute-start | bytes 49160 | tf_op jit(solution)/shard_map/ppermute | solution.py:33
  8.3 0.8 multiply_convert_fusion
  9.1 0.7 and_compare_fusion.6
  10.4 0.9 broadcast_multiply_fusion
  12.2 32.9 %all_gather.6 = bf16[24,64,256]{2,1,0:T(8,128)(2,1)S(1)} all-gather(bf16[24,8,256]{2,1,0:T(8,128)(2,1)S(1)} %fusion.49), channel_id=1, replica_groups=mesh['parts'=2,'chan'=4,'grp'=2,'tpl'=2] {'chan','grp'}, dimensions={1}, use_global_device_ids=true | all-gather | bytes 884736 | tf_op jit(solution)/shard_map/all_gather | solution.py:36
  45.1 1.8 %copy.73 = bf16[24,64,256]{1,0,2:T(8,128)(2,1)} copy(bf16[24,64,256]{2,1,0:T(8,128)(2,1)S(1)} %all_gather.6) | data formatting | bytes 1572864
  46.9 9.8 %fusion.54 = (bf16[24,64,264]{1,0,2:T(8,128)(2,1)S(1)}, bf16[24,64,264]{1,0,2:T(8,128)(2,1)S(1)}, bf16[24,64,264]{1,0,2:T(8,128)(2,1)}, bf16[24,64,264]{1,0,2:T(...) fusion(bf16[24,64,256]{1,0,2:T(8,128)(2,1)} %copy.73), kind=kLoop, calls=%fused_computation.119 | loop fusion | bytes 7274496 | tf_op jit(solution)/shard_map/jit(_pad)/pad | solution.py:52
  56.7 1.5 %constant_dynamic-update-slice_fusion.7 = bf16[8,24,64,33,8]{2,1,4,0,3:T(8,128)(2,1)} fusion(bf16[1,24,64,33,8]{2,1,4,0,3:T(8,128)(2,1)S(1)} %bitcast.174), kind=kLoop, calls=%fused_computation.102 | loop fusion | bytes 2433024
  58.2 3.1 %constant_dynamic-update-slice_fusion.6 = bf16[8,24,64,33,8]{2,1,4,0,3:T(8,128)(2,1)} fusion(bf16[8,24,64,33,8]{2,1,4,0,3:T(8,128)(2,1)} %constant_dynamic-update-slice_fusion.7, bf16[1,24,64,33,8]{2,1,4,0,3:T(8,128)(2,1)} %bitcast.173), kind=kLoop, calls=%fused_computation.101 | loop fusion | bytes 3244032
  61.3 2.9 %constant_dynamic-update-slice_fusion.5 = bf16[8,24,64,33,8]{2,1,4,0,3:T(8,128)(2,1)} fusion(bf16[8,24,64,33,8]{2,1,4,0,3:T(8,128)(2,1)} %constant_dynamic-update-slice_fusion.6, bf16[1,24,64,33,8]{2,1,4,0,3:T(8,128)(2,1)} %bitcast.172), kind=kLoop, calls=%fused_computation.100 | loop fusion | bytes 3244032
  64.2 2.9 %constant_dynamic-update-slice_fusion.4 = bf16[8,24,64,33,8]{2,1,4,0,3:T(8,128)(2,1)} fusion(bf16[8,24,64,33,8]{2,1,4,0,3:T(8,128)(2,1)} %constant_dynamic-update-slice_fusion.5, bf16[1,24,64,33,8]{2,1,4,0,3:T(8,128)(2,1)} %bitcast.171), kind=kLoop, calls=%fused_computation.99 | loop fusion | bytes 3244032
  67.1 1.5 %constant_dynamic-update-slice_fusion.3 = bf16[8,24,64,33,8]{2,1,4,0,3:T(8,128)(2,1)} fusion(bf16[8,24,64,33,8]{2,1,4,0,3:T(8,128)(2,1)} %constant_dynamic-update-slice_fusion.4, bf16[1,24,64,33,8]{2,1,4,0,3:T(8,128)(2,1)S(1)} %bitcast.170), kind=kLoop, calls=%fused_computation.98 | loop fusion | bytes 2433024
  68.7 1.5 %constant_dynamic-update-slice_fusion.2 = bf16[8,24,64,33,8]{2,1,4,0,3:T(8,128)(2,1)} fusion(bf16[8,24,64,33,8]{2,1,4,0,3:T(8,128)(2,1)} %constant_dynamic-update-slice_fusion.3, bf16[1,24,64,33,8]{2,1,4,0,3:T(8,128)(2,1)S(1)} %bitcast.169), kind=kLoop, calls=%fused_computation.97 | loop fusion | bytes 2433024
  70.1 1.5 %constant_dynamic-update-slice_fusion.1 = bf16[8,24,64,33,8]{2,1,4,0,3:T(8,128)(2,1)} fusion(bf16[8,24,64,33,8]{2,1,4,0,3:T(8,128)(2,1)} %constant_dynamic-update-slice_fusion.2, bf16[1,24,64,33,8]{2,1,4,0,3:T(8,128)(2,1)S(1)} %bitcast.168), kind=kLoop, calls=%fused_computation.96 | loop fusion | bytes 2433024
  71.7 1.5 %constant_dynamic-update-slice_fusion = bf16[8,24,64,33,8]{2,1,4,0,3:T(8,128)(2,1)} fusion(bf16[8,24,64,33,8]{2,1,4,0,3:T(8,128)(2,1)} %constant_dynamic-update-slice_fusion.1, bf16[1,24,64,33,8]{2,1,4,0,3:T(8,128)(2,1)S(1)} %bitcast.167), kind=kLoop, calls=%fused_computation.95 | loop fusion | bytes 2433024 | tf_op jit(solution)/shard_map/stack | solution.py:52
  73.2 1.5 %select_reduce_fusion = bf16[256,128]{1,0:T(8,128)(2,1)S(1)} fusion(f32[32]{0:T(128)S(1)} %convert_element_type.46, s32[256,128]{1,0:T(8,128)S(1)} %iota_subtract_fusion), kind=kLoop, calls=%fused_computation.2 | loop fusion | flops 3112960 | bytes 196736 | tf_op jit(solution)/shard_map/reduce_sum | solution.py:17
  74.7 1.0 pad_maximum_fusion
  75.7 0.2 reshape.85
  75.9 0.2 fusion.55
  76.2 0.3 fusion.5
  76.5 0.4 copy.64
  76.9 0.5 copy.66
  77.4 0.1 fusion.9
  77.6 20.4 %psum.7 = f32[64,1]{0,1:T(1,128)S(1)} all-reduce(f32[64,1]{0,1:T(1,128)S(1)} %bitcast.177), channel_id=1, replica_groups=mesh['parts'=2,'chan'=4,'grp'=2,'tpl'=2] {'chan','grp'}, use_global_device_ids=true, to_apply=%region_2.3 | all-reduce | flops 64 | bytes 512 | tf_op jit(solution)/shard_map/psum | solution.py:44
  98.0 0.2 select_convert_fusion
  98.2 0.1 fusion.41
  98.3 0.1 fusion.40
  98.5 0.1 fusion.39
  98.6 0.1 fusion.38
  98.8 0.1 fusion.37
  98.9 0.1 fusion.36
  99.0 0.1 fusion.35
  99.2 0.1 fusion.34
  99.3 0.1 fusion.33
  99.5 0.1 fusion.32
  99.6 0.1 fusion.31
  99.8 0.1 fusion.30
  99.9 0.1 fusion.29
  100.1 0.1 fusion.28
  100.2 0.1 fusion.27
  100.4 0.1 fusion.26
  100.5 0.1 fusion.25
  100.7 0.1 fusion.24
  100.8 0.1 fusion.23
  101.0 0.1 fusion.22
  101.1 0.1 fusion.21
  101.3 0.1 fusion.20
  101.4 0.1 fusion.19
  101.6 0.1 fusion.18
  101.7 0.1 fusion.17
  101.9 0.1 fusion.16
  102.0 0.1 fusion.15
  102.2 0.1 fusion.14
  102.3 0.1 fusion.13
  102.5 0.1 fusion.12
  102.6 0.1 fusion.11
  102.8 0.1 fusion.10
  102.9 3.7 %fusion.2 = f32[24,256,8]{1,0,2:T(8,128)S(1)} fusion(bf16[8,24,64,33,8]{2,1,4,0,3:T(8,128)(2,1)S(1)} %copy-done.2, bf16[64,33,256,8]{2,0,3,1:T(8,128)(2,1)S(1)} %fusion.10), kind=kOutput, calls=%fused_computation.4 | convolution fusion | flops 1660944384 | bytes 15335424 | tf_op jit(solution)/shard_map/cjbs,rkcjs->kbr/dot_general | solution.py:54
  106.6 0.4 copy.67
  107.0 15.5 %all_gather.7 = f32[24,4096]{0,1:T(8,128)S(1)} all-gather(f32[24,2048]{0,1:T(8,128)S(1)} %bitcast.176), channel_id=1, replica_groups=mesh['parts'=2,'chan'=4,'grp'=2,'tpl'=2] {'grp'}, dimensions={1}, use_global_device_ids=true | all-gather | bytes 589824 | tf_op jit(solution)/shard_map/all_gather | solution.py:65
  122.5 1.3 %copy.68 = f32[24,4096]{1,0:T(8,128)} copy(f32[24,4096]{0,1:T(8,128)S(1)} %all_gather.7) | data formatting | bytes 786432 | tf_op jit(solution)/shard_map/all_gather | solution.py:65
  (35 shorter events, 1.8 us)
Async XLA Ops:
  0.8 73.9 %collective-permute-start.1 = (bf16[64,256]{1,0:T(8,128)(2,1)S(1)}, bf16[64,256]{1,0:T(8,128)(2,1)S(1)}, u32[]{:S(2)}, u32[]{:S(2)}) collective-permute-start(bf16[64,256]{1,0:T(8,128)(2,1)S(1)} %slice.143), channel_id=1, source_target_pairs={{2,0},{4,2},{6,4},{8,6},{10,8},{12,10},{14,12},{3,1},{5,3},{7,5},{... | collective-permute-start | bytes 98312 | tf_op jit(solution)/shard_map/ppermute | solution.py:34
  2.8 71.9 %collective-permute-start = (bf16[64,128]{1,0:T(8,128)(2,1)S(1)}, bf16[64,128]{1,0:T(8,128)(2,1)S(1)}, u32[]{:S(2)}, u32[]{:S(2)}) collective-permute-start(bf16[64,128]{1,0:T(8,128)(2,1)S(1)} %slice.142), channel_id=1, source_target_pairs={{0,2},{2,4},{4,6},{6,8},{8,10},{10,12},{12,14},{1,3},{3,5},{5,7},{... | collective-permute-start | bytes 49160 | tf_op jit(solution)/shard_map/ppermute | solution.py:33
  46.9 11.3 %copy-start.3 = (bf16[32]{0:T(256)(128)(2,1)S(1)}, bf16[32]{0:T(256)(128)(2,1)}, u32[]{:S(2)}) copy-start(bf16[32]{0:T(256)(128)(2,1)} %param.7) | copy-start | bytes 196
  58.2 8.9 %copy-start.1 = (bf16[24,64,264]{1,0,2:T(8,128)(2,1)S(1)}, bf16[24,64,264]{1,0,2:T(8,128)(2,1)}, u32[]{:S(2)}) copy-start(bf16[24,64,264]{1,0,2:T(8,128)(2,1)} %get-tuple-element.8) | copy-start | bytes 2433028
  58.2 10.4 %copy-start = (bf16[24,64,264]{1,0,2:T(8,128)(2,1)S(1)}, bf16[24,64,264]{1,0,2:T(8,128)(2,1)}, u32[]{:S(2)}) copy-start(bf16[24,64,264]{1,0,2:T(8,128)(2,1)} %get-tuple-element.7) | copy-start | bytes 2433028
  98.1 4.8 %copy-start.2 = (bf16[8,24,64,33,8]{2,1,4,0,3:T(8,128)(2,1)S(1)}, bf16[8,24,64,33,8]{2,1,4,0,3:T(8,128)(2,1)}, u32[]{:S(2)}) copy-start(bf16[8,24,64,33,8]{2,1,4,0,3:T(8,128)(2,1)} %constant_dynamic-update-slice_fusion) | copy-start | bytes 19464196

commit v2 on v1

--- a/solution.py
+++ b/solution.py
@@ -1,6 +1,10 @@
+import functools
+
 import jax
 import jax.numpy as jnp
 from jax import lax
+from jax.experimental import pallas as pl
+from jax.experimental.pallas import tpu as pltpu
 from jax.sharding import PartitionSpec as P
 
 axes = ("chan", "grp")
@@ -24,6 +28,109 @@
         moved = jnp.pad(rows, ((0, 0), (0, 0), (1 << bit, 0)))[:, :, :extended]
         rows = jnp.where(((moveout >> bit) & 1)[:, :, None] == 1, moved, rows)
     return rows
+
+
+def gather_kernel(grp, count, tpl_ref, sum_ref, tpl_all, sum_all, send_sem, recv_sem, own_sem):
+    me = lax.axis_index("chan") * grp + lax.axis_index("grp")
+
+    def place(index):
+        return {"chan": index // grp, "grp": index % grp}
+
+    barrier = pltpu.get_barrier_semaphore()
+    for step in range(1, count):
+        pl.semaphore_signal(barrier, inc=1, device_id=place((me + step) % count), device_id_type=pl.DeviceIdType.MESH)
+    pl.semaphore_wait(barrier, count - 1)
+    sent = []
+    for kind, (src, dst) in enumerate(((sum_ref, sum_all), (tpl_ref, tpl_all))):
+        for step in range(1, count):
+            sent.append(pltpu.make_async_remote_copy(
+                src_ref=src,
+                dst_ref=dst.at[me],
+                send_sem=send_sem.at[kind, step],
+                recv_sem=recv_sem.at[kind, step],
+                device_id=place((me + step) % count),
+                device_id_type=pl.DeviceIdType.MESH,
+            ))
+            sent[-1].start()
+        kept = pltpu.make_async_copy(src, dst.at[me], own_sem.at[kind])
+        kept.start()
+        kept.wait()
+    for copy in sent:
+        copy.wait()
+
+
+def gather(tpl, sums, grp, count):
+    return pl.pallas_call(
+        functools.partial(gather_kernel, grp, count),
+        out_shape=(
+            jax.ShapeDtypeStruct((count,) + tpl.shape, tpl.dtype),
+            jax.ShapeDtypeStruct((count,) + sums.shape, sums.dtype),
+        ),
+        in_specs=[pl.BlockSpec(memory_space=pltpu.VMEM)] * 2,
+        out_specs=[pl.BlockSpec(memory_space=pltpu.VMEM)] * 2,
+        scratch_shapes=[
+            pltpu.SemaphoreType.DMA((2, count)),
+            pltpu.SemaphoreType.DMA((2, count)),
+            pltpu.SemaphoreType.DMA((2,)),
+        ],
+        compiler_params=pltpu.CompilerParams(collective_id=0, has_side_effects=True, vmem_limit_bytes=24 << 20),
+    )(tpl, sums)
+
+
+def correlate_kernel(wave_ref, tpl_ref, out_ref):
+    steps = out_ref.shape[0]
+    width = wave_ref.shape[1]
+    total = jnp.zeros(out_ref.shape, jnp.float32)
+    for j in range(lags // stride):
+        left = wave_ref[j:j + steps, :].astype(jnp.bfloat16)
+        start = width * (j + 1)
+        right = jnp.concatenate(
+            [tpl_ref[:, start - 128 * r:start - 128 * r + width] for r in range(stride // 2)], axis=0
+        )
+        total = total + lax.dot_general(left, right, (((1,), (1,)), ((), ())), preferred_element_type=jnp.float32)
+    out_ref[...] = total
+
+
+def packed(records, fir, templates, channel_sel, moveout, alive, chan, grp):
+    chans, length = records.shape
+    tpl_count = templates.shape[0]
+    count = chan * grp
+    me = lax.axis_index(axes)
+    before = lax.ppermute(records[:, length - 128:], axes, [(i, i + 1) for i in range(count - 1)])
+    after = lax.ppermute(records[:, :extended], axes, [(i + 1, i) for i in range(count - 1)])
+    shifted = shift_templates(templates, channel_sel, moveout, alive)
+    signal = jnp.concatenate([before, records, after], axis=1)
+    total = length + extended
+    blocks = signal.reshape(chans, total // 128 + 1, 128)
+    paired = jnp.concatenate([blocks[:, :-1], blocks[:, 1:]], axis=2)
+    filtered = jnp.einsum("cbi,ir->cbr", paired, filter_matrix(fir), preferred_element_type=jnp.float32)
+    filtered = filtered.reshape(chans, total)
+    own = filtered[:, :length]
+    sums = jnp.broadcast_to(jnp.pad(jnp.sum(own * own, axis=1), (0, 128 - chans))[None], (8, 128))
+    rows = shifted.reshape(-1, extended)
+    tpl_all, sum_all = gather(rows, sums, grp, count)
+    power = jnp.sum(sum_all[:, 0, :chans], axis=0)[:, None] / (length * count)
+    inside = (jnp.arange(total) < length) | (me < count - 1)
+    whitened = jnp.where(inside[None], filtered * lax.rsqrt(power + small_eps), 0.0).astype(jnp.bfloat16)
+    wave = whitened.astype(jnp.float32).T.reshape(total // stride, stride * chans)
+    tpl = tpl_all.reshape(count, tpl_count, chans // count, extended).transpose(1, 3, 0, 2)
+    tpl = jnp.pad(tpl.reshape(tpl_count, extended * chans), ((0, 32 - tpl_count), (0, 0)))
+    room = stride * chans
+    tpl = jnp.concatenate(
+        [jnp.pad(tpl, ((0, 0), (room, room))), jnp.pad(tpl, ((0, 0), (room + chans, room - chans)))], axis=0
+    )
+    steps = length // stride
+    out = pl.pallas_call(
+        correlate_kernel,
+        out_shape=jax.ShapeDtypeStruct((steps, 32 * stride), jnp.float32),
+        in_specs=[pl.BlockSpec(memory_space=pltpu.VMEM)] * 2,
+        out_specs=pl.BlockSpec(memory_space=pltpu.VMEM),
+        compiler_params=pltpu.CompilerParams(vmem_limit_bytes=32 << 20),
+    )(wave, tpl)
+    stack = out.reshape(steps, stride, 32)[:, :, :tpl_count].transpose(2, 0, 1).reshape(tpl_count, length)
+    other = lax.ppermute(stack, "grp", [(0, 1), (1, 0)])
+    first = lax.axis_index("grp") == 0
+    return jnp.concatenate([jnp.where(first, stack, other), jnp.where(first, other, stack)], axis=1)
 
 
 def time_split(records, fir, templates, channel_sel, moveout, alive, chan, grp):
@@ -69,6 +176,9 @@
     chan, grp = mesh.shape["chan"], mesh.shape["grp"]
 
     def body(*args):
+        chans, tpl_count = args[0].shape[0], args[2].shape[0]
+        if chans == 64 and tpl_count <= 32 and grp == 2:
+            return packed(*args, chan, grp)
         return time_split(*args, chan, grp)
 
     in_specs = (

time: 124 us -> 62.9 us (0.51)
  the two profiles are of different devices: /device:TPU:0 before, /device:TPU:14 now
where the time goes in v2:
time: 62.9 us; the launch traced here: 62.5 us
  Pallas kernels  24.3 us (39%)
  local copies, waits for them, and re-layouts  16.9 us (27%)
  other arithmetic  7.94 us (13%)
  waiting for transfers between devices  6.77 us (11%)
  starting transfers between devices  5.87 us (9%)
    pallas_call x1, Pallas kernels, gather(): pl.pallas_call(functools.partial(gather_kernel, grp, count), out_shape=(j...  21.9 us
    reshape x1, local copies, waits for them, and re-layouts, packed(): tpl_all.reshape(count, tpl_count, chans // count, extended)  6.88 us
    ppermute x1, waiting for transfers between devices, packed(): other = lax.ppermute(stack, 'grp', [(0, 1), (1, 0)])  6.77 us
    reshape x1, local copies, waits for them, and re-layouts, packed(): tpl.reshape(tpl_count, extended * chans)  3.46 us
    ppermute x1, starting transfers between devices, packed(): lax.ppermute(records[:, length - 128:], axes, [(i, i + 1) for i in range(...  3.44 us
    pallas_call x1, Pallas kernels, packed(): pl.pallas_call(correlate_kernel, out_shape=jax.ShapeDtypeStruct((steps, 3...  2.44 us
    ppermute x1, starting transfers between devices, packed(): lax.ppermute(records[:, :extended], axes, [(i + 1, i) for i in range(coun...  2.37 us
    select_n x1, local copies, waits for them, and re-layouts, packed(): jnp.where(first, stack, other)  1.52 us
  transfers between devices with their start and end apart: 3, of which 1 were waited for; matrix products, arithmetic and copies ran while one was open for 11% of the time, Pallas kernels for 0%

profile of v2, /device:TPU:14, one launch (start us, length us, event | category | flops | bytes accessed | tf_op | source)
XLA Modules:
  0.0 62.5 jit_solution(1491796212579775088)
XLA Ops:
  0.0 0.0 copy-start
  0.0 0.8 %slice.42 = bf16[64,128]{1,0:T(8,128)(2,1)S(1)} slice(bf16[64,2048]{1,0:T(8,128)(2,1)} %param.6), slice={[0:64], [1920:2048]} | slice | bytes 32768 | tf_op jit(solution)/shard_map/slice | solution.py:99
  0.8 3.4 %collective-permute-start = (bf16[64,128]{1,0:T(8,128)(2,1)S(1)}, bf16[64,128]{1,0:T(8,128)(2,1)S(1)}, u32[]{:S(2)}, u32[]{:S(2)}) collective-permute-start(bf16[64,128]{1,0:T(8,128)(2,1)S(1)} %slice.42), channel_id=1, source_target_pairs={{0,2},{2,4},{4,6},{6,8},{8,10},{10,12},{12,14},{1,3},{3,5},{5,7},{... | collective-permute-start | bytes 49160 | tf_op jit(solution)/shard_map/ppermute | solution.py:99
  4.2 0.8 %slice.43 = bf16[64,256]{1,0:T(8,128)(2,1)S(1)} slice(bf16[64,2048]{1,0:T(8,128)(2,1)} %param.6), slice={[0:64], [0:256]} | slice | bytes 65536 | tf_op jit(solution)/shard_map/slice | solution.py:100
  5.0 2.4 %collective-permute-start.1 = (bf16[64,256]{1,0:T(8,128)(2,1)S(1)}, bf16[64,256]{1,0:T(8,128)(2,1)S(1)}, u32[]{:S(2)}, u32[]{:S(2)}) collective-permute-start(bf16[64,256]{1,0:T(8,128)(2,1)S(1)} %slice.43), channel_id=1, source_target_pairs={{2,0},{4,2},{6,4},{8,6},{10,8},{12,10},{14,12},{3,1},{5,3},{7,5},{... | collective-permute-start | bytes 98312 | tf_op jit(solution)/shard_map/ppermute | solution.py:100
  7.4 0.7 %convert_element_type.37 = f32[32]{0:T(128)S(1)} convert(bf16[32]{0:T(256)(128)(2,1)} %param.7) | non-fusion elementwise | flops 32 | bytes 192 | tf_op jit(solution)/shard_map/convert_element_type | solution.py:21
  8.1 0.8 %multiply_convert_fusion = bf16[24,8]{0,1:T(8,128)(2,1)S(1)} fusion(s32[24,8]{0,1:T(8,128)} %param.9, s32[8]{0:T(128)} %param.11), kind=kLoop, calls=%fused_computation.43 | loop fusion | flops 384 | bytes 1184 | tf_op jit(solution)/shard_map/convert_element_type | solution.py:25
  8.8 0.1 copy.65
  8.9 0.7 %and_compare_fusion.6 = (pred[24,8]{0,1:T(8,128)(4,1)S(1)}, pred[24,8]{0,1:T(8,128)(4,1)S(1)}, pred[24,8]{0,1:T(8,128)(4,1)S(1)}, pred[24,8]{0,1:T(8,128)(4,1)S(...) fusion(s32[24,8]{0,1:T(8,128)} %param.10), kind=kLoop, calls=%fused_computation.50 | loop fusion | flops 4032 | bytes 2112 | tf_op jit(solution)/shard_map/eq | solution.py:29
  9.6 0.1 copy.58
  9.7 0.1 copy.62
  9.8 0.1 copy.61
  9.9 0.1 copy.60
  10.0 0.1 copy.59
  10.1 0.1 copy.64
  10.2 0.1 copy.63
  10.3 0.9 %broadcast_multiply_fusion = bf16[24,8,128]{2,1,0:T(8,128)(2,1)S(1)} fusion(bf16[24,8,128]{2,1,0:T(8,128)(2,1)} %param.8, bf16[24,8]{1,0:T(8,128)(2,1)S(1)} %copy.65), kind=kLoop, calls=%fused_computation.39 | loop fusion | flops 24576 | bytes 98688 | tf_op jit(solution)/shard_map/mul | solution.py:26
  11.2 0.1 fusion.7
  11.3 0.1 fusion.8
  11.5 0.1 fusion.9
  11.6 0.1 fusion.10
  11.7 0.1 fusion.11
  11.8 0.1 fusion.12
  12.0 0.1 fusion.14.tpl_ref
  12.1 1.5 %select_reduce_fusion = bf16[256,128]{1,0:T(8,128)(2,1)S(1)} fusion(f32[32]{0:T(128)S(1)} %convert_element_type.37, s32[256,128]{1,0:T(8,128)S(1)} %iota_subtract_fusion), kind=kLoop, calls=%fused_computation.4 | loop fusion | flops 3112960 | bytes 196736 | tf_op jit(solution)/shard_map/reduce_sum | solution.py:21
  13.6 0.0 collective-permute-done
  13.6 0.0 collective-permute-done.1
  13.6 0.0 copy-done
  13.6 0.2 reshape.80
  13.8 0.2 fusion.19
  14.0 0.1 copy.76
  14.1 0.1 copy.77
  14.2 0.3 convolution_bitcast_fusion
  14.5 0.1 fusion.6
  14.7 21.9 %shard_map.64 = (bf16[8,192,256]{2,1,0:T(8,128)(2,1)S(1)}, f32[8,8,128]{2,1,0:T(8,128)S(1)}) custom-call(bf16[192,256]{1,0:T(8,128)(2,1)S(1)} %fusion.14.tpl_ref, f32[8,128]{1,0:T(8,128)S(1)} %broadcast_in_dim.89.sum_ref), custom_call_target="tpu_custom_call" | custom-call | tf_op jit(solution)/shard_map/pallas_call | solution.py:63
  36.6 0.1 convert_bitcast_fusion
  36.7 0.4 copy.66
  37.1 0.3 reshape.90.wave_ref
  37.4 6.9 %copy.67 = bf16[8,24,8,256]{1,2,0,3:T(8,128)(2,1)} copy(bf16[8,24,8,256]{3,2,1,0:T(8,128)(2,1)S(1)} %bitcast.24) | data formatting | bytes 1572864 | tf_op jit(solution)/shard_map/reshape | solution.py:116
  44.3 3.5 %copy.68 = bf16[24,16384]{1,0:T(8,128)(2,1)S(1)} copy(bf16[24,16384]{0,1:T(8,128)(2,1)} %bitcast.25) | data formatting | bytes 1572864 | tf_op jit(solution)/shard_map/reshape | solution.py:117
  47.8 0.1 pad.57
  47.8 0.4 fusion.2.tpl_ref
  48.2 2.4 %shard_map.65 = f32[256,256]{1,0:T(8,128)S(1)} custom-call(f32[288,512]{1,0:T(8,128)S(1)} %reshape.90.wave_ref, bf16[64,17408]{1,0:T(8,128)(2,1)S(1)} %fusion.2.tpl_ref), custom_call_target="tpu_custom_call" | custom-call | tf_op jit(solution)/shard_map/pallas_call | solution.py:123
  50.7 0.1 copy.69
  50.8 0.4 copy.70
  51.2 0.3 copy.71
  51.5 0.1 collective-permute-start.2
  51.6 6.8 %collective-permute-done.2 = f32[24,2048]{1,0:T(8,128)S(1)} collective-permute-done((f32[24,2048]{1,0:T(8,128)S(1)}, f32[24,2048]{1,0:T(8,128)S(1)}, u32[]{:S(2)}, u32[]{:S(2)}) %collective-permute-start.2) | collective-permute-done | bytes 196640 | tf_op jit(solution)/shard_map/ppermute | solution.py:131
  58.4 0.3 copy.72
  58.7 1.1 %broadcast_select_fusion.1 = (f32[24,2048]{0,1:T(8,128)}, f32[24,2048]{0,1:T(8,128)S(1)}) fusion(f32[24,2048]{0,1:T(8,128)S(1)} %copy.72, pred[]{:T(512)S(6)} %eq.44, f32[24,256,8]{0,2,1:T(8,128)S(1)} %copy.70), kind=kLoop, calls=%fused_computation.17 | loop fusion | flops 98304 | bytes 786433 | tf_op jit(solution)/shard_map/jit(_where)/select_n | solution.py:133
  59.8 1.5 %copy.74 = f32[24,2048]{1,0:T(8,128)S(1)} copy(f32[24,2048]{0,1:T(8,128)} %get-tuple-element.9) | data formatting | bytes 393216 | tf_op jit(solution)/shard_map/jit(_where)/select_n | solution.py:133
  61.4 0.3 copy.75
  61.7 0.8 %pad_maximum_fusion = f32[24,4096]{1,0:T(8,128)} fusion(f32[24,2048]{1,0:T(8,128)S(1)} %copy.75, f32[24,2048]{1,0:T(8,128)S(1)} %copy.74), kind=kLoop, calls=%fused_computation.18 | loop fusion | flops 98304 | bytes 786432 | tf_op jit(solution)/shard_map/concatenate | solution.py:133
  (11 shorter events, 0.2 us)
Async XLA Ops:
  0.0 13.6 %copy-start = (bf16[64,2048]{1,0:T(8,128)(2,1)S(1)}, bf16[64,2048]{1,0:T(8,128)(2,1)}, u32[]{:S(2)}) copy-start(bf16[64,2048]{1,0:T(8,128)(2,1)} %param.6) | copy-start | bytes 786436
  0.8 12.8 %collective-permute-start = (bf16[64,128]{1,0:T(8,128)(2,1)S(1)}, bf16[64,128]{1,0:T(8,128)(2,1)S(1)}, u32[]{:S(2)}, u32[]{:S(2)}) collective-permute-start(bf16[64,128]{1,0:T(8,128)(2,1)S(1)} %slice.42), channel_id=1, source_target_pairs={{0,2},{2,4},{4,6},{6,8},{8,10},{10,12},{12,14},{1,3},{3,5},{5,7},{... | collective-permute-start | bytes 49160 | tf_op jit(solution)/shard_map/ppermute | solution.py:99
  5.0 8.6 %collective-permute-start.1 = (bf16[64,256]{1,0:T(8,128)(2,1)S(1)}, bf16[64,256]{1,0:T(8,128)(2,1)S(1)}, u32[]{:S(2)}, u32[]{:S(2)}) collective-permute-start(bf16[64,256]{1,0:T(8,128)(2,1)S(1)} %slice.43), channel_id=1, source_target_pairs={{2,0},{4,2},{6,4},{8,6},{10,8},{12,10},{14,12},{3,1},{5,3},{7,5},{... | collective-permute-start | bytes 98312 | tf_op jit(solution)/shard_map/ppermute | solution.py:100
  51.5 6.8 %collective-permute-start.2 = (f32[24,2048]{1,0:T(8,128)S(1)}, f32[24,2048]{1,0:T(8,128)S(1)}, u32[]{:S(2)}, u32[]{:S(2)}) collective-permute-start(f32[24,2048]{1,0:T(8,128)S(1)} %copy.71), channel_id=1, source_target_pairs={{0,2},{2,0},{1,3},{3,1},{4,6},{6,4},{5,7},{7,5},{8,10},{10,8},{9,1... | collective-permute-start | bytes 589832 | tf_op jit(solution)/shard_map/ppermute | solution.py:131

commit v3 on v2

--- a/solution.py
+++ b/solution.py
@@ -130,7 +130,9 @@
     stack = out.reshape(steps, stride, 32)[:, :, :tpl_count].transpose(2, 0, 1).reshape(tpl_count, length)
     other = lax.ppermute(stack, "grp", [(0, 1), (1, 0)])
     first = lax.axis_index("grp") == 0
-    return jnp.concatenate([jnp.where(first, stack, other), jnp.where(first, other, stack)], axis=1)
+    return jnp.where(
+        first, jnp.concatenate([stack, other], axis=1), jnp.concatenate([other, stack], axis=1)
+    )
 
 
 def time_split(records, fir, templates, channel_sel, moveout, alive, chan, grp):

time: 62.9 us -> 59.6 us (0.948)
  local copies, waits for them, and re-layouts: 16.9 us -> 14.8 us
  other arithmetic: 7.94 us -> 6.81 us
    select_n x2 -> x0, local copies, waits for them, and re-layouts: 1.83 us -> none  [the longest x1 1.52 us: packed(): jnp.where(first, stack, other)]
    concatenate x1 -> x0, other arithmetic: 0.78 us -> none  [packed(): jnp.concatenate([jnp.where(first, stack, other), jnp.where(first, other,...]
  transfers between devices with their start and end apart: 3 -> 3, of which waited for: 1 -> 1; matrix products, arithmetic and copies ran while one was open for 11% -> 12% of each run, Pallas kernels for 0% -> 0%
where the time goes in v3:
time: 59.6 us; the launch traced here: 59.1 us
  Pallas kernels  24.3 us (41%)
  local copies, waits for them, and re-layouts  14.8 us (25%)
  other arithmetic  6.81 us (11%)
  waiting for transfers between devices  6.77 us (11%)
  starting transfers between devices  5.87 us (10%)
    pallas_call x1, Pallas kernels, gather(): pl.pallas_call(functools.partial(gather_kernel, grp, count), out_shape=(j...  21.9 us
    reshape x1, local copies, waits for them, and re-layouts, packed(): tpl_all.reshape(count, tpl_count, chans // count, extended)  6.88 us
    ppermute x1, waiting for transfers between devices, packed(): other = lax.ppermute(stack, 'grp', [(0, 1), (1, 0)])  6.77 us
    reshape x1, local copies, waits for them, and re-layouts, packed(): tpl.reshape(tpl_count, extended * chans)  3.46 us
    ppermute x1, starting transfers between devices, packed(): lax.ppermute(records[:, length - 128:], axes, [(i, i + 1) for i in range(...  3.44 us
    pallas_call x1, Pallas kernels, packed(): pl.pallas_call(correlate_kernel, out_shape=jax.ShapeDtypeStruct((steps, 3...  2.44 us
    ppermute x1, starting transfers between devices, packed(): lax.ppermute(records[:, :extended], axes, [(i + 1, i) for i in range(coun...  2.37 us
    reduce_sum x1, other arithmetic, filter_matrix(): jnp.sum(jnp.where(hits, fir.astype(jnp.float32), 0.0), axis=2)  1.47 us
  transfers between devices with their start and end apart: 3, of which 1 were waited for; matrix products, arithmetic and copies ran while one was open for 12% of the time, Pallas kernels for 0%

profile of v3, /device:TPU:14, one launch (start us, length us, event | category | flops | bytes accessed | tf_op | source)
XLA Modules:
  0.0 59.1 jit_solution(2901855010200676800)
XLA Ops:
  0.0 0.0 copy-start
  0.0 0.8 %slice.42 = bf16[64,128]{1,0:T(8,128)(2,1)S(1)} slice(bf16[64,2048]{1,0:T(8,128)(2,1)} %param.6), slice={[0:64], [1920:2048]} | slice | bytes 32768 | tf_op jit(solution)/shard_map/slice | solution.py:99
  0.8 3.4 %collective-permute-start = (bf16[64,128]{1,0:T(8,128)(2,1)S(1)}, bf16[64,128]{1,0:T(8,128)(2,1)S(1)}, u32[]{:S(2)}, u32[]{:S(2)}) collective-permute-start(bf16[64,128]{1,0:T(8,128)(2,1)S(1)} %slice.42), channel_id=1, source_target_pairs={{0,2},{2,4},{4,6},{6,8},{8,10},{10,12},{12,14},{1,3},{3,5},{5,7},{... | collective-permute-start | bytes 49160 | tf_op jit(solution)/shard_map/ppermute | solution.py:99
  4.2 0.8 %slice.43 = bf16[64,256]{1,0:T(8,128)(2,1)S(1)} slice(bf16[64,2048]{1,0:T(8,128)(2,1)} %param.6), slice={[0:64], [0:256]} | slice | bytes 65536 | tf_op jit(solution)/shard_map/slice | solution.py:100
  5.0 2.4 %collective-permute-start.1 = (bf16[64,256]{1,0:T(8,128)(2,1)S(1)}, bf16[64,256]{1,0:T(8,128)(2,1)S(1)}, u32[]{:S(2)}, u32[]{:S(2)}) collective-permute-start(bf16[64,256]{1,0:T(8,128)(2,1)S(1)} %slice.43), channel_id=1, source_target_pairs={{2,0},{4,2},{6,4},{8,6},{10,8},{12,10},{14,12},{3,1},{5,3},{7,5},{... | collective-permute-start | bytes 98312 | tf_op jit(solution)/shard_map/ppermute | solution.py:100
  7.4 0.7 %convert_element_type.37 = f32[32]{0:T(128)S(1)} convert(bf16[32]{0:T(256)(128)(2,1)} %param.7) | non-fusion elementwise | flops 32 | bytes 192 | tf_op jit(solution)/shard_map/convert_element_type | solution.py:21
  8.1 0.8 %multiply_convert_fusion = bf16[24,8]{0,1:T(8,128)(2,1)S(1)} fusion(s32[24,8]{0,1:T(8,128)} %param.9, s32[8]{0:T(128)} %param.11), kind=kLoop, calls=%fused_computation.41 | loop fusion | flops 384 | bytes 1184 | tf_op jit(solution)/shard_map/convert_element_type | solution.py:25
  8.8 0.1 copy.63
  8.9 0.7 %and_compare_fusion.6 = (pred[24,8]{0,1:T(8,128)(4,1)S(1)}, pred[24,8]{0,1:T(8,128)(4,1)S(1)}, pred[24,8]{0,1:T(8,128)(4,1)S(1)}, pred[24,8]{0,1:T(8,128)(4,1)S(...) fusion(s32[24,8]{0,1:T(8,128)} %param.10), kind=kLoop, calls=%fused_computation.48 | loop fusion | flops 4032 | bytes 2112 | tf_op jit(solution)/shard_map/eq | solution.py:29
  9.6 0.1 copy.56
  9.7 0.1 copy.60
  9.8 0.1 copy.59
  9.9 0.1 copy.58
  10.0 0.1 copy.57
  10.1 0.1 copy.62
  10.2 0.1 copy.61
  10.3 0.9 %broadcast_multiply_fusion = bf16[24,8,128]{2,1,0:T(8,128)(2,1)S(1)} fusion(bf16[24,8,128]{2,1,0:T(8,128)(2,1)} %param.8, bf16[24,8]{1,0:T(8,128)(2,1)S(1)} %copy.63), kind=kLoop, calls=%fused_computation.37 | loop fusion | flops 24576 | bytes 98688 | tf_op jit(solution)/shard_map/mul | solution.py:26
  11.2 0.1 fusion.7
  11.3 0.1 fusion.8
  11.5 0.1 fusion.9
  11.6 0.1 fusion.10
  11.7 0.1 fusion.11
  11.8 0.1 fusion.12
  12.0 0.1 fusion.14.tpl_ref
  12.1 1.5 %select_reduce_fusion = bf16[256,128]{1,0:T(8,128)(2,1)S(1)} fusion(f32[32]{0:T(128)S(1)} %convert_element_type.37, s32[256,128]{1,0:T(8,128)S(1)} %iota_subtract_fusion), kind=kLoop, calls=%fused_computation.4 | loop fusion | flops 3112960 | bytes 196736 | tf_op jit(solution)/shard_map/reduce_sum | solution.py:21
  13.6 0.0 collective-permute-done
  13.6 0.0 collective-permute-done.1
  13.6 0.0 copy-done
  13.6 0.2 reshape.80
  13.8 0.2 fusion.19
  14.0 0.1 copy.72
  14.1 0.1 copy.73
  14.2 0.3 convolution_bitcast_fusion
  14.5 0.1 fusion.6
  14.7 21.9 %shard_map.64 = (bf16[8,192,256]{2,1,0:T(8,128)(2,1)S(1)}, f32[8,8,128]{2,1,0:T(8,128)S(1)}) custom-call(bf16[192,256]{1,0:T(8,128)(2,1)S(1)} %fusion.14.tpl_ref, f32[8,128]{1,0:T(8,128)S(1)} %broadcast_in_dim.89.sum_ref), custom_call_target="tpu_custom_call" | custom-call | tf_op jit(solution)/shard_map/pallas_call | solution.py:63
  36.6 0.1 convert_bitcast_fusion
  36.7 0.4 copy.64
  37.1 0.3 reshape.90.wave_ref
  37.4 6.9 %copy.65 = bf16[8,24,8,256]{1,2,0,3:T(8,128)(2,1)} copy(bf16[8,24,8,256]{3,2,1,0:T(8,128)(2,1)S(1)} %bitcast.22) | data formatting | bytes 1572864 | tf_op jit(solution)/shard_map/reshape | solution.py:116
  44.3 3.5 %copy.66 = bf16[24,16384]{1,0:T(8,128)(2,1)S(1)} copy(bf16[24,16384]{0,1:T(8,128)(2,1)} %bitcast.23) | data formatting | bytes 1572864 | tf_op jit(solution)/shard_map/reshape | solution.py:117
  47.8 0.1 pad.57
  47.8 0.4 fusion.2.tpl_ref
  48.2 2.4 %shard_map.65 = f32[256,256]{1,0:T(8,128)S(1)} custom-call(f32[288,512]{1,0:T(8,128)S(1)} %reshape.90.wave_ref, bf16[64,17408]{1,0:T(8,128)(2,1)S(1)} %fusion.2.tpl_ref), custom_call_target="tpu_custom_call" | custom-call | tf_op jit(solution)/shard_map/pallas_call | solution.py:123
  50.7 0.1 copy.67
  50.8 0.4 copy.68
  51.2 0.3 copy.70
  51.5 0.1 collective-permute-start.2
  51.6 6.8 %collective-permute-done.2 = f32[24,2048]{1,0:T(8,128)S(1)} collective-permute-done((f32[24,2048]{1,0:T(8,128)S(1)}, f32[24,2048]{1,0:T(8,128)S(1)}, u32[]{:S(2)}, u32[]{:S(2)}) %collective-permute-start.2) | collective-permute-done | bytes 196640 | tf_op jit(solution)/shard_map/ppermute | solution.py:131
  58.4 0.8 %maximum_select_fusion = f32[24,4096]{1,0:T(8,128)} fusion(f32[24,2048]{1,0:T(8,128)S(1)} %collective-permute-done.2, f32[24,2048]{1,0:T(8,128)S(1)} %copy.70, pred[]{:T(512)S(6)} %eq.44), kind=kLoop, calls=%fused_computation.16 | loop fusion | flops 294912 | bytes 786433 | tf_op jit(solution)/shard_map/jit(_where)/select_n | solution.py:133
  (11 shorter events, 0.2 us)
Async XLA Ops:
  0.0 13.6 %copy-start = (bf16[64,2048]{1,0:T(8,128)(2,1)S(1)}, bf16[64,2048]{1,0:T(8,128)(2,1)}, u32[]{:S(2)}) copy-start(bf16[64,2048]{1,0:T(8,128)(2,1)} %param.6) | copy-start | bytes 786436
  0.8 12.8 %collective-permute-start = (bf16[64,128]{1,0:T(8,128)(2,1)S(1)}, bf16[64,128]{1,0:T(8,128)(2,1)S(1)}, u32[]{:S(2)}, u32[]{:S(2)}) collective-permute-start(bf16[64,128]{1,0:T(8,128)(2,1)S(1)} %slice.42), channel_id=1, source_target_pairs={{0,2},{2,4},{4,6},{6,8},{8,10},{10,12},{12,14},{1,3},{3,5},{5,7},{... | collective-permute-start | bytes 49160 | tf_op jit(solution)/shard_map/ppermute | solution.py:99
  5.0 8.6 %collective-permute-start.1 = (bf16[64,256]{1,0:T(8,128)(2,1)S(1)}, bf16[64,256]{1,0:T(8,128)(2,1)S(1)}, u32[]{:S(2)}, u32[]{:S(2)}) collective-permute-start(bf16[64,256]{1,0:T(8,128)(2,1)S(1)} %slice.43), channel_id=1, source_target_pairs={{2,0},{4,2},{6,4},{8,6},{10,8},{12,10},{14,12},{3,1},{5,3},{7,5},{... | collective-permute-start | bytes 98312 | tf_op jit(solution)/shard_map/ppermute | solution.py:100
  51.5 6.8 %collective-permute-start.2 = (f32[24,2048]{1,0:T(8,128)S(1)}, f32[24,2048]{1,0:T(8,128)S(1)}, u32[]{:S(2)}, u32[]{:S(2)}) collective-permute-start(f32[24,2048]{1,0:T(8,128)S(1)} %copy.70), channel_id=1, source_target_pairs={{0,2},{2,0},{1,3},{3,1},{4,6},{6,4},{5,7},{7,5},{8,10},{10,8},{9,1... | collective-permute-start | bytes 589832 | tf_op jit(solution)/shard_map/ppermute | solution.py:131
